TPU v7x, 32 devices: a whole 2x2x4 slice. The times are simulated.
32 devices in a mesh: dp: 8 (over y, x, core), mp: 4 (over z).
Axes of the slice: x: 2, y: 2, z: 4, core: 2. Of those that a mesh axis runs over, the one named last changes fastest.
Arguments:
- tokens: bfloat16 [16384, 768], P(('dp', 'mp')), may hold values from -6 to 6
- segments: int32 [8, 2048], P('dp'), may hold values from -1 to 2048, as said below
- out_grad: bfloat16 [16384, 768], P(('dp', 'mp')), may hold values from -6 to 6
- align_grad: bfloat16 [16384, 1024], P(('dp', 'mp')), may hold values from -6 to 6
- first_gain: bfloat16 [768], P(('dp', 'mp')), may hold values from 0.5 to 1.5
- first_shift: bfloat16 [768], P(('dp', 'mp')), may hold values from -1.75 to 1.75
- joint_weight: bfloat16 [768, 2304], P(('dp', 'mp')), may hold values from -0.21875 to 0.21875
- query_bias: bfloat16 [768], P(('dp', 'mp')), may hold values from -3 to 3
- value_bias: bfloat16 [768], P(('dp', 'mp')), may hold values from -3 to 3
- output_weight: bfloat16 [768, 768], P(('dp', 'mp')), may hold values from -0.875 to 0.875
- output_bias: bfloat16 [768], P(('dp', 'mp')), may hold values from -1.75 to 1.75
- second_gain: bfloat16 [768], P(('dp', 'mp')), may hold values from 0.5 to 1.5
- second_shift: bfloat16 [768], P(('dp', 'mp')), may hold values from -1.75 to 1.75
- expand_bias: bfloat16 [3072], P(('dp', 'mp')), may hold values from -3 to 3
- reduce_bias: bfloat16 [768], P(('dp', 'mp')), may hold values from -1.75 to 1.75
- head_gain: bfloat16 [768], P(('dp', 'mp')), may hold values from 0.5 to 1.5
- head_shift: bfloat16 [768], P(('dp', 'mp')), may hold values from -1.75 to 1.75
- align_weight: bfloat16 [768, 1024], P(('dp', 'mp')), may hold values from -0.21875 to 0.21875
- align_bias: bfloat16 [1024], P(('dp', 'mp')), may hold values from -3 to 3
- expand_weight: bfloat16 [768, 3072], P('dp', 'mp'), may hold values from -0.21875 to 0.21875
- reduce_weight: bfloat16 [3072, 768], P('mp', 'dp'), may hold values from -0.109375 to 0.109375
Outputs:
- block_out: bfloat16 [16384, 768], P(('dp', 'mp'))
- align_out: bfloat16 [16384, 1024], P(('dp', 'mp'))
- tokens_grad: float32 [16384, 768], P(('dp', 'mp'))
- first_gain_grad: float32 [768], P(('dp', 'mp'))
- first_shift_grad: float32 [768], P(('dp', 'mp'))
- joint_weight_grad: float32 [768, 2304], P(('dp', 'mp'))
- query_bias_grad: float32 [768], P(('dp', 'mp'))
- value_bias_grad: float32 [768], P(('dp', 'mp'))
- output_weight_grad: float32 [768, 768], P(('dp', 'mp'))
- output_bias_grad: float32 [768], P(('dp', 'mp'))
- second_gain_grad: float32 [768], P(('dp', 'mp'))
- second_shift_grad: float32 [768], P(('dp', 'mp'))
- expand_bias_grad: float32 [3072], P(('dp', 'mp'))
- reduce_bias_grad: float32 [768], P(('dp', 'mp'))
- head_gain_grad: float32 [768], P(('dp', 'mp'))
- head_shift_grad: float32 [768], P(('dp', 'mp'))
- align_weight_grad: float32 [768, 1024], P(('dp', 'mp'))
- align_bias_grad: float32 [1024], P(('dp', 'mp'))
- expand_weight_grad: float32 [768, 3072], P('dp', 'mp')
- reduce_weight_grad: float32 [3072, 768], P('mp', 'dp')
Inputs may be any that keep to these rules, and one draw needn't show every extreme that they name: `segments`: segment numbers never fall along a row; padding slots carry -1 and stand at the end of a row, every row having some; the last segment before the padding is numbered 2048 in every row; in every row one segment starts within the first 256 slots and ends after slot 1536.
All inputs are finite; a program needn't handle non-finite values.
Results may differ from a plain program's by a relative error of at most 0.014.
Values may be sent and summed in bfloat16 or wider, within the bound.
A program may use at most 192 MiB of HBM per device.

v0:
```python
import math

import jax
import jax.numpy as jnp
from jax import lax
from jax.sharding import PartitionSpec as P

H = 12
HD = 64
FF = 3072


EPSILON = 1e-06
NEG_FILL = -1000000000.0


def layer_norm(values, gain, shift):
    centre = values - jnp.mean(values, axis=-1, keepdims=True)
    spread = jnp.mean(centre * centre, axis=-1, keepdims=True)
    return centre * lax.rsqrt(spread + EPSILON) * gain + shift


def exact_gelu(values):
    return jax.nn.gelu(values, approximate=False)


def matmul(left, right):
    return jnp.dot(left, right, preferred_element_type=jnp.float32)


def left_product(left, right):
    return jnp.einsum("ti,to->io", left, right, preferred_element_type=jnp.float32)


def right_product(left, right):
    return jnp.einsum("to,io->ti", left, right, preferred_element_type=jnp.float32)


def column_sums(values):
    return jnp.sum(values.astype(jnp.float32), axis=0)


def local(
    tokens,
    segments,
    out_grad,
    align_grad,
    first_gain,
    first_shift,
    joint_weight,
    query_bias,
    value_bias,
    output_weight,
    output_bias,
    second_gain,
    second_shift,
    expand_bias,
    reduce_bias,
    head_gain,
    head_shift,
    align_weight,
    align_bias,
    expand_weight,
    reduce_weight,
):
    gathered = (
        lax.all_gather(first_gain, ("dp", "mp"), axis=0, tiled=True),
        lax.all_gather(first_shift, ("dp", "mp"), axis=0, tiled=True),
        lax.all_gather(joint_weight, ("dp", "mp"), axis=0, tiled=True),
        lax.all_gather(query_bias, ("dp", "mp"), axis=0, tiled=True),
        lax.all_gather(value_bias, ("dp", "mp"), axis=0, tiled=True),
        lax.all_gather(output_weight, ("dp", "mp"), axis=0, tiled=True),
        lax.all_gather(output_bias, ("dp", "mp"), axis=0, tiled=True),
        lax.all_gather(second_gain, ("dp", "mp"), axis=0, tiled=True),
        lax.all_gather(second_shift, ("dp", "mp"), axis=0, tiled=True),
        lax.all_gather(expand_bias, ("dp", "mp"), axis=0, tiled=True),
        lax.all_gather(reduce_bias, ("dp", "mp"), axis=0, tiled=True),
        lax.all_gather(head_gain, ("dp", "mp"), axis=0, tiled=True),
        lax.all_gather(head_shift, ("dp", "mp"), axis=0, tiled=True),
        lax.all_gather(align_weight, ("dp", "mp"), axis=0, tiled=True),
        lax.all_gather(align_bias, ("dp", "mp"), axis=0, tiled=True),
    )
    (
        gain_one,
        shift_one,
        joint_full,
        bias_query,
        bias_value,
        output_full,
        bias_output,
        gain_two,
        shift_two,
        bias_expand,
        bias_reduce,
        gain_head,
        shift_head,
        align_full,
        bias_align,
    ) = gathered
    (
        gain_one,
        shift_one,
        bias_query,
        bias_value,
        bias_output,
        gain_two,
        shift_two,
        bias_expand,
        bias_reduce,
        gain_head,
        shift_head,
        bias_align,
    ) = tuple(
        (
            vector.astype(jnp.float32)
            for vector in (
                gain_one,
                shift_one,
                bias_query,
                bias_value,
                bias_output,
                gain_two,
                shift_two,
                bias_expand,
                bias_reduce,
                gain_head,
                shift_head,
                bias_align,
            )
        )
    )
    expand_local, reduce_local = (
        lax.all_gather(expand_weight, "dp", axis=0, tiled=True),
        lax.all_gather(reduce_weight, "dp", axis=1, tiled=True),
    )
    own_rows = tokens.shape[0]
    model_width = tokens.shape[1]
    mp_index = lax.axis_index("mp")
    seq_len = own_rows * lax.axis_size("mp")
    hidden_cols = expand_local.shape[1]
    score_scale = 1.0 / math.sqrt(HD)
    segment_all = segments[0]
    segment_own = lax.dynamic_slice_in_dim(segment_all, mp_index * own_rows, own_rows)
    resid = tokens.astype(jnp.float32)
    normed_one = layer_norm(resid, gain_one, shift_one).astype(jnp.bfloat16)
    joint_bias = jnp.concatenate([bias_query, jnp.zeros_like(bias_query), bias_value])
    projected = (matmul(normed_one, joint_full) + joint_bias).astype(jnp.bfloat16)
    key_values = lax.all_gather(projected[:, model_width:], "mp", axis=0, tiled=True)
    queries = projected[:, :model_width].reshape(own_rows, H, HD)
    block_len = min(512, seq_len)
    block_count = seq_len // block_len
    key_blocks = key_values[:, :model_width].reshape(block_count, block_len, H, HD)
    value_blocks = key_values[:, model_width:].reshape(block_count, block_len, H, HD)
    segment_blocks = segment_all.reshape(block_count, block_len)

    def scores(key_block, segment_block):
        logits = (
            jnp.einsum("qhd,khd->hqk", queries, key_block, preferred_element_type=jnp.float32)
            * score_scale
        )
        allowed = (segment_own[:, None] == segment_block[None, :])[None]
        return (logits, allowed)

    def max_step(carry, item):
        running_max, running_sum = carry
        key_block, segment_block = item
        logits, allowed = scores(key_block, segment_block)
        logits = jnp.where(allowed, logits, NEG_FILL)
        new_max = jnp.maximum(running_max, jnp.max(logits, axis=-1))
        running_sum = running_sum * jnp.exp(running_max - new_max) + jnp.sum(
            jnp.exp(logits - new_max[..., None]), axis=-1
        )
        return ((new_max, running_sum), None)

    start_max = jnp.full((H, own_rows), NEG_FILL, jnp.float32)
    (final_max, final_sum), _ = lax.scan(
        max_step, (start_max, jnp.zeros((H, own_rows), jnp.float32)), (key_blocks, segment_blocks)
    )
    log_total = final_max + jnp.log(final_sum)

    def softmax_rows(key_block, segment_block):
        logits, allowed = scores(key_block, segment_block)
        return jnp.where(allowed, jnp.exp(logits - log_total[..., None]), 0.0)

    def output_step(accumulated, item):
        key_block, value_block, segment_block = item
        weights_low = softmax_rows(key_block, segment_block).astype(jnp.bfloat16)
        return (
            accumulated
            + jnp.einsum(
                "hqk,khd->qhd", weights_low, value_block, preferred_element_type=jnp.float32
            ),
            None,
        )

    attended, _ = lax.scan(
        output_step,
        jnp.zeros((own_rows, H, HD), jnp.float32),
        (key_blocks, value_blocks, segment_blocks),
    )
    attended_low = attended.reshape(own_rows, model_width).astype(jnp.bfloat16)
    middle = resid + matmul(attended_low, output_full) + bias_output
    normed_two = layer_norm(middle, gain_two, shift_two).astype(jnp.bfloat16)
    feed_input = lax.all_gather(normed_two, "mp", axis=0, tiled=True)
    expand_part = lax.dynamic_slice_in_dim(bias_expand, mp_index * hidden_cols, hidden_cols)
    preactivation = matmul(feed_input, expand_local) + expand_part
    activated = exact_gelu(preactivation).astype(jnp.bfloat16)
    feed_out = lax.psum_scatter(
        matmul(activated, reduce_local).astype(jnp.bfloat16), "mp", scatter_dimension=0, tiled=True
    ).astype(jnp.float32)
    block_out = middle + feed_out + bias_reduce
    normed_three = layer_norm(block_out, gain_head, shift_head).astype(jnp.bfloat16)
    align_out = matmul(normed_three, align_full) + bias_align
    grad_align_w = left_product(normed_three, align_grad)
    grad_align_b = column_sums(align_grad)
    back_three = right_product(align_grad, align_full)
    _, norm_pull = jax.vjp(layer_norm, block_out, gain_head, shift_head)
    back_extra, grad_head_gain, grad_head_shift = norm_pull(back_three)
    back_block = out_grad.astype(jnp.float32) + back_extra
    back_feed = back_block.astype(jnp.bfloat16)
    grad_reduce_b = column_sums(back_feed)
    feed_grads = lax.all_gather(back_feed, "mp", axis=0, tiled=True)
    reduce_grad_part = left_product(activated, feed_grads)
    back_active = right_product(feed_grads, reduce_local)
    _, gelu_pull = jax.vjp(exact_gelu, preactivation)
    back_pre = gelu_pull(back_active)[0].astype(jnp.bfloat16)
    expand_grad_part = left_product(feed_input, back_pre)
    grad_expand_b = lax.dynamic_update_slice_in_dim(
        jnp.zeros((FF,), jnp.float32), column_sums(back_pre), mp_index * hidden_cols, 0
    )
    back_two = lax.psum_scatter(
        right_product(back_pre, expand_local).astype(jnp.bfloat16),
        "mp",
        scatter_dimension=0,
        tiled=True,
    ).astype(jnp.float32)
    grad_expand_w, grad_reduce_w = (
        lax.psum_scatter(expand_grad_part, "dp", scatter_dimension=0, tiled=True),
        lax.psum_scatter(reduce_grad_part, "dp", scatter_dimension=1, tiled=True),
    )
    _, norm_pull = jax.vjp(layer_norm, middle, gain_two, shift_two)
    middle_extra, grad_second_gain, grad_second_shift = norm_pull(back_two)
    back_middle = back_block + middle_extra
    back_output = back_middle.astype(jnp.bfloat16)
    grad_output_b = column_sums(back_output)
    grad_output_w = left_product(attended_low, back_output)
    back_attended = (
        right_product(back_output, output_full).astype(jnp.bfloat16).reshape(own_rows, H, HD)
    )
    row_terms = jnp.einsum("qhd,qhd->hq", back_attended.astype(jnp.float32), attended)

    def backward_step(query_grad, item):
        key_block, value_block, segment_block = item
        weights_full = softmax_rows(key_block, segment_block)
        weights_low = weights_full.astype(jnp.bfloat16)
        value_grad = jnp.einsum(
            "hqk,qhd->khd", weights_low, back_attended, preferred_element_type=jnp.float32
        )
        weight_grad = jnp.einsum(
            "qhd,khd->hqk", back_attended, value_block, preferred_element_type=jnp.float32
        )
        logit_grad = (weights_full * (weight_grad - row_terms[..., None])).astype(jnp.bfloat16)
        query_grad = (
            query_grad
            + jnp.einsum("hqk,khd->qhd", logit_grad, key_block, preferred_element_type=jnp.float32)
            * score_scale
        )
        key_grad = (
            jnp.einsum("hqk,qhd->khd", logit_grad, queries, preferred_element_type=jnp.float32)
            * score_scale
        )
        return (query_grad, (key_grad, value_grad))

    query_grad, (key_grads, value_grads) = lax.scan(
        backward_step,
        jnp.zeros((own_rows, H, HD), jnp.float32),
        (key_blocks, value_blocks, segment_blocks),
    )
    key_own, value_own = (
        lax.psum_scatter(
            key_grads.reshape(seq_len, model_width).astype(jnp.bfloat16),
            "mp",
            scatter_dimension=0,
            tiled=True,
        ).astype(jnp.float32),
        lax.psum_scatter(
            value_grads.reshape(seq_len, model_width).astype(jnp.bfloat16),
            "mp",
            scatter_dimension=0,
            tiled=True,
        ).astype(jnp.float32),
    )
    back_joint = jnp.concatenate(
        [query_grad.reshape(own_rows, model_width), key_own, value_own], axis=1
    ).astype(jnp.bfloat16)
    grad_query_b = column_sums(back_joint[:, :model_width])
    grad_value_b = column_sums(back_joint[:, 2 * model_width :])
    grad_joint_w = left_product(normed_one, back_joint)
    back_one = right_product(back_joint, joint_full)
    _, norm_pull = jax.vjp(layer_norm, resid, gain_one, shift_one)
    input_extra, grad_first_gain, grad_first_shift = norm_pull(back_one)
    tokens_grad = back_middle + input_extra
    (
        g_first_gain,
        g_first_shift,
        g_joint,
        g_query,
        g_value,
        g_output_w,
        g_output_b,
        g_second_gain,
        g_second_shift,
        g_expand_b,
        g_reduce_b,
        g_head_gain,
        g_head_shift,
        g_align_w,
        g_align_b,
    ) = (
        lax.psum_scatter(grad_first_gain, ("dp", "mp"), scatter_dimension=0, tiled=True),
        lax.psum_scatter(grad_first_shift, ("dp", "mp"), scatter_dimension=0, tiled=True),
        lax.psum_scatter(grad_joint_w, ("dp", "mp"), scatter_dimension=0, tiled=True),
        lax.psum_scatter(grad_query_b, ("dp", "mp"), scatter_dimension=0, tiled=True),
        lax.psum_scatter(grad_value_b, ("dp", "mp"), scatter_dimension=0, tiled=True),
        lax.psum_scatter(grad_output_w, ("dp", "mp"), scatter_dimension=0, tiled=True),
        lax.psum_scatter(grad_output_b, ("dp", "mp"), scatter_dimension=0, tiled=True),
        lax.psum_scatter(grad_second_gain, ("dp", "mp"), scatter_dimension=0, tiled=True),
        lax.psum_scatter(grad_second_shift, ("dp", "mp"), scatter_dimension=0, tiled=True),
        lax.psum_scatter(grad_expand_b, ("dp", "mp"), scatter_dimension=0, tiled=True),
        lax.psum_scatter(grad_reduce_b, ("dp", "mp"), scatter_dimension=0, tiled=True),
        lax.psum_scatter(grad_head_gain, ("dp", "mp"), scatter_dimension=0, tiled=True),
        lax.psum_scatter(grad_head_shift, ("dp", "mp"), scatter_dimension=0, tiled=True),
        lax.psum_scatter(grad_align_w, ("dp", "mp"), scatter_dimension=0, tiled=True),
        lax.psum_scatter(grad_align_b, ("dp", "mp"), scatter_dimension=0, tiled=True),
    )
    return (
        block_out.astype(jnp.bfloat16),
        align_out.astype(jnp.bfloat16),
        tokens_grad,
        g_first_gain,
        g_first_shift,
        g_joint,
        g_query,
        g_value,
        g_output_w,
        g_output_b,
        g_second_gain,
        g_second_shift,
        g_expand_b,
        g_reduce_b,
        g_head_gain,
        g_head_shift,
        g_align_w,
        g_align_b,
        grad_expand_w,
        grad_reduce_w,
    )


def solution(mesh):
    in_specs = (
        P(("dp", "mp"), None),
        P("dp", None),
        P(("dp", "mp"), None),
        P(("dp", "mp"), None),
        P(("dp", "mp")),
        P(("dp", "mp")),
        P(("dp", "mp"), None),
        P(("dp", "mp")),
        P(("dp", "mp")),
        P(("dp", "mp"), None),
        P(("dp", "mp")),
        P(("dp", "mp")),
        P(("dp", "mp")),
        P(("dp", "mp")),
        P(("dp", "mp")),
        P(("dp", "mp")),
        P(("dp", "mp")),
        P(("dp", "mp"), None),
        P(("dp", "mp")),
        P("dp", "mp"),
        P("mp", "dp"),
    )
    out_specs = (
        P(("dp", "mp"), None),
        P(("dp", "mp"), None),
        P(("dp", "mp"), None),
        P(("dp", "mp")),
        P(("dp", "mp")),
        P(("dp", "mp"), None),
        P(("dp", "mp")),
        P(("dp", "mp")),
        P(("dp", "mp"), None),
        P(("dp", "mp")),
        P(("dp", "mp")),
        P(("dp", "mp")),
        P(("dp", "mp")),
        P(("dp", "mp")),
        P(("dp", "mp")),
        P(("dp", "mp")),
        P(("dp", "mp"), None),
        P(("dp", "mp")),
        P("dp", "mp"),
        P("mp", "dp"),
    )
    return jax.shard_map(local, mesh=mesh, in_specs=in_specs, out_specs=out_specs, check_vma=False)
```

profile of v0, /device:TPU:0, one launch (start us, length us, event | category | flops | bytes accessed | tf_op | source)
XLA Modules:
  0.0 1386.4 jit_solution(6732463906286537332)
XLA Ops:
  18.0 43.1 %all-reduce.25 = (bf16[768]{0:T(1024)(128)(2,1)S(1)}, bf16[768]{0:T(1024)(128)(2,1)S(1)}, bf16[768]{0:T(1024)(128)(2,1)S(1)}, bf16[768]{0:T(1024)(128)(2,1)S(1)}...) all-reduce(bf16[768]{0:T(1024)(128)(2,1)S(1)} %dynamic-update-slice, ...), channel_id=1, replica_groups=mesh['dp'=8,'mp'=4] {'dp','mp'}, use_global_device_ids=true, to_apply=%add.3 | all-reduce | flops 11776 | bytes 47104
  64.6 9.3 all-gather.9.cloned.1.call-done
  85.3 110.2 %all-gather.11.cloned.1.call-done = bf16[2048,1536]{1,0:T(8,128)(2,1)} async-done(((bf16[512,1536]{1,0:T(8,128)(2,1)}), bf16[2048,1536]{1,0:T(8,128)(2,1)}) %all-gather.11.cloned.1.call-update) | async-done | bytes 6291472 | tf_op jit(solution)/shard_map/all_gather | solution.py:148
  216.8 61.0 %while.39 = (s32[]{:T(128)}, f32[12,512]{1,0:T(8,128)S(1)}, f32[12,512]{1,0:T(8,128)S(1)}, s32[512]{0:T(512)S(1)}, s32[4,512]{1,0:T(4,128)S(1)}, /*index=5*/bf16...) while((s32[]{:T(128)}, f32[12,512]{1,0:T(8,128)S(1)}, ...), condition=%wide.region_5.6_spmd.clone, body=%wide.region_2.5_spmd.clone.sunk | while | flops 424966144 | bytes 27853420 | solution.py:176
  293.0 27.2 %while.40 = (s32[]{:T(128)}, f32[512,12,64]{0,2,1:T(8,128)}, bf16[4,512,12,64]{1,3,2,0:T(8,128)(2,1)}, s32[512]{0:T(512)S(1)}, s32[4,512]{1,0:T(4,128)S(1)}, /*i...) while((s32[]{:T(128)}, f32[512,12,64]{0,2,1:T(8,128)}, ...), condition=%wide.region_7.8_spmd.clone, body=%wide.region_6.7_spmd.clone.sunk | while | flops 818937856 | bytes 6063219 | solution.py:196
  327.4 61.1 %all-gather.15.cloned.1.call-done = bf16[2048,768]{1,0:T(8,128)(2,1)} async-done(((bf16[512,768]{1,0:T(8,128)(2,1)}), bf16[2048,768]{1,0:T(8,128)(2,1)}) %all-gather.15.cloned.1.call-update) | async-done | bytes 3145744 | tf_op jit(solution)/shard_map/all_gather | solution.py:204
  388.4 18.9 %multiply_convert_fusion = (bf16[2048,768]{1,0:T(8,128)(2,1)}, f32[2048,768]{1,0:T(8,128)}, f32[2048,768]{1,0:T(8,128)}) fusion(f32[768]{0:T(1024)S(1)} %dynamic-slice_convert_fusion, bf16[2048,768]{1,0:T(8,128)(2,1)} %all-gather.15.cloned.1.call-done, bf16[768,768]{1,0:T(8,128)(2,1)} %all-gather.17.cloned.1.call-done), kind=kOutput, calls=%fused_computation.54 | convolution fusion | flops 2519728128 | bytes 20057088 | tf_op jit(solution)/shard_map/dot_general | solution.py:28
  420.3 59.6 %reduce-scatter.10.cloned.1.call-done = bf16[512,768]{1,0:T(8,128)(2,1)} async-done(((bf16[2048,768]{1,0:T(8,128)(2,1)}), bf16[512,768]{1,0:T(8,128)(2,1)}) %reduce-scatter.10.cloned.1.call-update) | async-done | bytes 786448 | tf_op jit(solution)/shard_map/reduce_scatter | solution.py:208
  482.8 55.1 %all-gather.21.cloned.1.call-done = bf16[768,1024]{1,0:T(8,128)(2,1)} async-done(((bf16[24,1024]{1,0:T(8,128)(2,1)}), bf16[768,1024]{1,0:T(8,128)(2,1)}) %all-gather.21.cloned.1.call-update) | async-done | bytes 1572880 | tf_op jit(solution)/shard_map/all_gather | solution.py:80
  546.8 62.1 %all-gather.23.cloned.1.call-done = bf16[2048,768]{1,0:T(8,128)(2,1)} async-done(((bf16[512,768]{1,0:T(8,128)(2,1)}), bf16[2048,768]{1,0:T(8,128)(2,1)}) %all-gather.23.cloned.1.call-update) | async-done | bytes 3145744 | tf_op jit(solution)/shard_map/all_gather | solution.py:222
  608.9 11.1 convert_reduce_fusion
  625.8 59.0 %reduce-scatter.12.cloned.1.call-done = bf16[512,768]{1,0:T(8,128)(2,1)} async-done(((bf16[2048,768]{1,0:T(8,128)(2,1)}), bf16[512,768]{1,0:T(8,128)(2,1)}) %reduce-scatter.12.cloned.1.call-update) | async-done | bytes 786448 | tf_op jit(solution)/shard_map/reduce_scatter | solution.py:231
  695.2 124.3 %while.41 = (s32[]{:T(128)}, f32[512,12,64]{0,2,1:T(8,128)}, bf16[4,512,12,64]{1,3,2,0:T(8,128)(2,1)}, bf16[4,512,12,64]{1,3,2,0:T(8,128)(2,1)}, bf16[4,512,12,6...) while((s32[]{:T(128)}, f32[512,12,64]{0,2,1:T(8,128)}, ...), condition=%wide.region_19.20_spmd.clone, body=%wide.region_18.19_spmd.clone.sunk | while | flops 2046558208 | bytes 151079712 | solution.py:274
  748.9 8.2 bitcast_dynamic-update-slice_fusion.5
  780.0 8.2 bitcast_dynamic-update-slice_fusion.5
  811.1 8.2 bitcast_dynamic-update-slice_fusion.5
  857.7 29.3 %reduce-scatter.14.cloned.1.call-done = bf16[512,768]{0,1:T(8,128)(2,1)} async-done(((bf16[2048,768]{0,1:T(8,128)(2,1)}), bf16[512,768]{0,1:T(8,128)(2,1)}) %reduce-scatter.14.cloned.1.call-update) | async-done | bytes 786448 | tf_op jit(solution)/shard_map/reduce_scatter | solution.py:280
  887.0 62.5 %reduce-scatter.16.cloned.1.call-done = bf16[512,768]{0,1:T(8,128)(2,1)} async-done(((bf16[2048,768]{0,1:T(8,128)(2,1)}), bf16[512,768]{0,1:T(8,128)(2,1)}) %reduce-scatter.16.cloned.1.call-update) | async-done | bytes 786448 | tf_op jit(solution)/shard_map/reduce_scatter | solution.py:286
  969.0 41.5 %all-reduce.24 = (f32[768]{0:T(1024)S(1)}, f32[768]{0:T(1024)S(1)}, f32[768]{0:T(1024)S(1)}, f32[768]{0:T(1024)S(1)}, f32[768]{0:T(1024)S(1)}, /*index=5*/f32[76...) all-reduce(f32[768]{0:T(1024)S(1)} %get-tuple-element.345, ...), channel_id=6, replica_groups=mesh['dp'=8,'mp'=4] {'dp','mp'}, use_global_device_ids=true, to_apply=%region_25.26.clone | all-reduce | flops 11776 | bytes 94208
  1020.6 36.9 %reduce-scatter.22.cloned.1.call-done = f32[24,1024]{1,0:T(8,128)} async-done(((f32[768,1024]{1,0:T(8,128)}), f32[24,1024]{1,0:T(8,128)}) %reduce-scatter.22.cloned.1.call-update) | async-done | bytes 98320 | tf_op jit(solution)/shard_map/reduce_scatter | solution.py:333
  1057.5 45.2 %reduce-scatter.26.cloned.1.call-done = f32[768,96]{0,1:T(8,128)} async-done(((f32[768,768]{0,1:T(8,128)}), f32[768,96]{0,1:T(8,128)}) %reduce-scatter.26.cloned.1.call-update) | async-done | bytes 294928 | tf_op jit(solution)/shard_map/reduce_scatter | solution.py:239
  1102.7 46.6 %reduce-scatter.24.cloned.1.call-done = f32[96,768]{1,0:T(8,128)} async-done(((f32[768,768]{1,0:T(8,128)}), f32[96,768]{1,0:T(8,128)}) %reduce-scatter.24.cloned.1.call-update) | async-done | bytes 294928 | tf_op jit(solution)/shard_map/reduce_scatter | solution.py:238
  1149.4 104.8 %reduce-scatter.20.cloned.1.call-done = f32[24,768]{1,0:T(8,128)} async-done(((f32[768,768]{1,0:T(8,128)}), f32[24,768]{1,0:T(8,128)}) %reduce-scatter.20.cloned.1.call-update) | async-done | bytes 73744 | tf_op jit(solution)/shard_map/reduce_scatter | solution.py:325
  1254.2 125.3 %reduce-scatter.18.cloned.1.call-done = f32[24,2304]{1,0:T(8,128)} async-done(((f32[768,2304]{1,0:T(8,128)}), f32[24,2304]{1,0:T(8,128)}) %reduce-scatter.18.cloned.1.call-update) | async-done | bytes 221200 | tf_op jit(solution)/shard_map/reduce_scatter | solution.py:322
  (339 shorter events, 364.1 us)
Async XLA Ops:
  7.2 66.8 %all-gather.9.cloned.1.call-start = ((), (), s32[]{:S(2)}) async-start(), calls=%async_computation.9 | async-start | bytes 3649536 | tf_op jit(solution)/shard_map/all_gather | solution.py:69
  7.9 187.6 %all-gather.11.cloned.1.call-start = ((), (), s32[]{:S(2)}) async-start(), calls=%async_computation.10 | async-start | bytes 7864320 | tf_op jit(solution)/shard_map/all_gather | solution.py:148
  81.2 241.5 %all-gather.13.cloned.1.call-start = ((), (), s32[]{:S(2)}) async-start(), calls=%async_computation.11 | async-start | bytes 1216512 | tf_op jit(solution)/shard_map/all_gather | solution.py:72
  81.9 245.4 %all-gather.17.cloned.1.call-start = ((), (), s32[]{:S(2)}) async-start(), calls=%async_computation.13 | async-start | bytes 1327104 | tf_op jit(solution)/shard_map/all_gather | solution.py:133
  82.5 305.9 %all-gather.15.cloned.1.call-start = ((), (), s32[]{:S(2)}) async-start(), calls=%async_computation.12 | async-start | bytes 3932160 | tf_op jit(solution)/shard_map/all_gather | solution.py:204
  293.0 29.6 %copy-start.12 = (bf16[512,768]{1,0:T(8,128)(2,1)S(1)}, bf16[512,768]{1,0:T(8,128)(2,1)}, u32[]{:S(2)}) copy-start(bf16[512,768]{1,0:T(8,128)(2,1)} %param.27) | copy-start | bytes 2359300
  326.7 86.3 %all-gather.19.cloned.1.call-start = ((), (), s32[]{:S(2)}) async-start(), calls=%async_computation.14 | async-start | bytes 1327104 | tf_op jit(solution)/shard_map/all_gather | solution.py:134
  327.2 152.7 %reduce-scatter.10.cloned.1.call-start = ((), (), s32[]{:S(2)}) async-start(), calls=%async_computation.15 | async-start | bytes 3932160 | tf_op jit(solution)/shard_map/reduce_scatter | solution.py:208
  419.5 118.4 %copy-start.20 = (bf16[512,1024]{1,0:T(8,128)(2,1)S(1)}, bf16[512,1024]{1,0:T(8,128)(2,1)}, u32[]{:S(2)}) copy-start(bf16[512,1024]{1,0:T(8,128)(2,1)} %param.30) | copy-start | bytes 3145732
  419.5 118.4 %all-gather.21.cloned.1.call-start = ((), (), s32[]{:S(2)}) async-start(), calls=%async_computation.16 | async-start | bytes 1622016 | tf_op jit(solution)/shard_map/all_gather | solution.py:80
  420.3 188.6 %all-gather.23.cloned.1.call-start = ((), (), s32[]{:S(2)}) async-start(), calls=%async_computation.17 | async-start | bytes 3932160 | tf_op jit(solution)/shard_map/all_gather | solution.py:222
  546.3 138.4 %reduce-scatter.12.cloned.1.call-start = ((), (), s32[]{:S(2)}) async-start(), calls=%async_computation.18 | async-start | bytes 3932160 | tf_op jit(solution)/shard_map/reduce_scatter | solution.py:231
  625.7 261.3 %reduce-scatter.14.cloned.1.call-start = ((), (), s32[]{:S(2)}) async-start(), calls=%async_computation.19 | async-start | bytes 3932160 | tf_op jit(solution)/shard_map/reduce_scatter | solution.py:280
  826.5 122.9 %reduce-scatter.16.cloned.1.call-start = ((), (), s32[]{:S(2)}) async-start(), calls=%async_computation.20 | async-start | bytes 3932160 | tf_op jit(solution)/shard_map/reduce_scatter | solution.py:286
  833.6 223.9 %reduce-scatter.22.cloned.1.call-start = ((), (), s32[]{:S(2)}) async-start(), calls=%async_computation.23 | async-start | bytes 3244032 | tf_op jit(solution)/shard_map/reduce_scatter | solution.py:333
  838.2 264.5 %reduce-scatter.26.cloned.1.call-start = ((), (), s32[]{:S(2)}) async-start(), calls=%async_computation.25 | async-start | bytes 2654208 | tf_op jit(solution)/shard_map/reduce_scatter | solution.py:239
  845.3 304.1 %reduce-scatter.24.cloned.1.call-start = ((), (), s32[]{:S(2)}) async-start(), calls=%async_computation.24 | async-start | bytes 2654208 | tf_op jit(solution)/shard_map/reduce_scatter | solution.py:238
  852.7 401.5 %reduce-scatter.20.cloned.1.call-start = ((), (), s32[]{:S(2)}) async-start(), calls=%async_computation.22 | async-start | bytes 2433024 | tf_op jit(solution)/shard_map/reduce_scatter | solution.py:325
  856.6 92.8 %copy-start.25 = (f32[768]{0:T(1024)S(1)}, f32[768]{0:T(1024)}, u32[]{:S(2)}) copy-start(f32[768]{0:T(1024)} %copy-done.24) | copy-start | bytes 9220
  856.6 92.8 %copy-start.27 = (f32[512]{0:T(512)S(1)}, f32[512]{0:T(512)}, u32[]{:S(2)}) copy-start(f32[512]{0:T(512)} %copy-done.26) | copy-start | bytes 6148
  856.6 92.8 %copy-start.29 = (f32[512]{0:T(512)S(1)}, f32[512]{0:T(512)}, u32[]{:S(2)}) copy-start(f32[512]{0:T(512)} %copy-done.28) | copy-start | bytes 6148
  856.6 92.8 %copy-start.39 = (f32[768]{0:T(1024)S(1)}, f32[768]{0:T(1024)}, u32[]{:S(2)}) copy-start(f32[768]{0:T(1024)} %copy-done.38) | copy-start | bytes 9220
  856.7 522.8 %reduce-scatter.18.cloned.1.call-start = ((), (), s32[]{:S(2)}) async-start(), calls=%async_computation.21 | async-start | bytes 7299072 | tf_op jit(solution)/shard_map/reduce_scatter | solution.py:322
  967.0 50.5 %copy-start.9 = (f32[512,768]{1,0:T(8,128)S(1)}, f32[512,768]{1,0:T(8,128)}, u32[]{:S(2)}) copy-start(f32[512,768]{1,0:T(8,128)} %copy-done.8) | copy-start | bytes 4718596
  (51 other events, 263.2 us)
Sparse Core Ops, SparseCore 0:
  10.8 63.0 all-gather.8
  81.3 114.1 all-gather.10
  198.3 52.3 all-gather.12
  252.4 22.9 all-gather.16
  326.8 61.6 all-gather.14
  390.2 22.6 all-gather.18
  419.6 60.2 reduce-scatter.9
  482.8 55.0 all-gather.20
  546.5 62.3 all-gather.22
  625.8 58.8 reduce-scatter.11
  826.6 60.2 reduce-scatter.13
  889.1 60.2 reduce-scatter.15
  955.4 102.0 reduce-scatter.21
  1061.3 41.3 reduce-scatter.25
  1106.9 42.4 reduce-scatter.23
  1155.1 99.0 reduce-scatter.19
  1261.2 118.1 reduce-scatter.17
where the time goes:
time: 1390 us
  waiting for transfers between devices  876 us (63%)
  matrix products  258 us (19%)
  local copies, waits for them, and re-layouts  94 us (7%)
  blocking collectives  84.6 us (6%)
  other arithmetic  56.6 us (4%)
  between operations  15.1 us (1%)
    reduce_scatter x1, waiting for transfers between devices, local(): lax.psum_scatter(grad_joint_w, ('dp', 'mp'), scatter_dimension=0, tiled=T...  125 us
    all_gather x1, waiting for transfers between devices, local(): lax.all_gather(projected[:, model_width:], 'mp', axis=0, tiled=True)  110 us
    reduce_scatter x1, waiting for transfers between devices, local(): lax.psum_scatter(grad_output_w, ('dp', 'mp'), scatter_dimension=0, tiled=...  105 us
    unnamed x2, blocking collectives  84.6 us
    reduce_scatter x1, waiting for transfers between devices, local(): lax.psum_scatter(value_grads.reshape(seq_len, model_width).astype(jnp.bfl...  62.5 us
    all_gather x1, waiting for transfers between devices, local(): feed_grads = lax.all_gather(back_feed, 'mp', axis=0, tiled=True)  62.1 us
    all_gather x1, waiting for transfers between devices, local(): feed_input = lax.all_gather(normed_two, 'mp', axis=0, tiled=True)  61.1 us
    reduce_scatter x1, waiting for transfers between devices, local(): lax.psum_scatter(matmul(activated, reduce_local).astype(jnp.bfloat16), 'm...  59.6 us
  transfers between devices with their start and end apart: 17, of which 15 were waited for; matrix products, arithmetic and copies ran while one was open for 16% of the time, Pallas kernels for 0%

commit v1 on v0

v1 whole, which is shorter than its diff:
```python
import functools

import jax
import jax.numpy as jnp
from jax import lax
from jax.experimental import pallas as pl
from jax.experimental.pallas import tpu as pltpu
from jax.sharding import PartitionSpec as P

H = 12
HD = 64
EPSILON = 1e-06
NEG_FILL = -1000000000.0
MESH = pl.DeviceIdType.MESH
VMEM_LIMIT = 56 << 20


def layer_norm(values, gain, shift):
    centre = values - jnp.mean(values, axis=-1, keepdims=True)
    spread = jnp.mean(centre * centre, axis=-1, keepdims=True)
    return centre * lax.rsqrt(spread + EPSILON) * gain + shift


def exact_gelu(values):
    return jax.nn.gelu(values, approximate=False)


def matmul(left, right):
    return jnp.dot(left, right, preferred_element_type=jnp.float32)


def left_product(left, right):
    return jnp.einsum("ti,to->io", left, right, preferred_element_type=jnp.float32)


def right_product(left, right):
    return jnp.einsum("to,io->ti", left, right, preferred_element_type=jnp.float32)


def column_sums(values):
    return jnp.sum(values.astype(jnp.float32), axis=0)


def nn(left, right):
    return lax.dot_general(
        left, right, (((1,), (0,)), ((), ())), preferred_element_type=jnp.float32
    )


def nt(left, right):
    return lax.dot_general(
        left, right, (((1,), (1,)), ((), ())), preferred_element_type=jnp.float32
    )


ANY = pl.BlockSpec(memory_space=pl.ANY)
VM = pl.BlockSpec(memory_space=pltpu.VMEM)


def line_gather_kernel(nz, own, out, send_right, send_left, recv, local_sem):
    dp, z = lax.axis_index("dp"), lax.axis_index("mp")
    has_left, has_right = z > 0, z < nz - 1
    left, right = jnp.maximum(z - 1, 0), jnp.minimum(z + 1, nz - 1)
    barrier = pltpu.get_barrier_semaphore()

    for off in range(1, nz):
        pl.semaphore_signal(
            barrier, inc=1, device_id=(dp, lax.rem(z + off, nz)), device_id_type=MESH
        )
    keep = pltpu.make_async_copy(own, out.at[z], local_sem)
    keep.start()

    pl.semaphore_wait(barrier, nz - 1)

    def to_right(step):
        chunk = jnp.maximum(z - step, 0)
        return pltpu.make_async_remote_copy(
            src_ref=own if step == 0 else out.at[chunk],
            dst_ref=out.at[chunk],
            send_sem=send_right.at[step],
            recv_sem=recv.at[chunk],
            device_id=(dp, right),
            device_id_type=MESH,
        )

    def to_left(step):
        chunk = jnp.minimum(z + step, nz - 1)
        return pltpu.make_async_remote_copy(
            src_ref=own if step == 0 else out.at[chunk],
            dst_ref=out.at[chunk],
            send_sem=send_left.at[step],
            recv_sem=recv.at[chunk],
            device_id=(dp, left),
            device_id_type=MESH,
        )

    for step in range(nz):
        if step > 0:

            @pl.when(z - step >= 0)
            def _():
                to_right(step).wait_recv()

            @pl.when(z + step <= nz - 1)
            def _():
                to_left(step).wait_recv()

        if step < nz - 1:

            @pl.when(has_right & (z - step >= 0))
            def _():
                to_right(step).start()

            @pl.when(has_left & (z + step <= nz - 1))
            def _():
                to_left(step).start()

    for step in range(nz - 1):

        @pl.when(has_right & (z - step >= 0))
        def _():
            to_right(step).wait_send()

        @pl.when(has_left & (z + step <= nz - 1))
        def _():
            to_left(step).wait_send()

    keep.wait()


def line_gather(own, nz, cid):
    return pl.pallas_call(
        functools.partial(line_gather_kernel, nz),
        out_shape=jax.ShapeDtypeStruct((nz,) + own.shape, own.dtype),
        in_specs=[ANY],
        out_specs=ANY,
        scratch_shapes=[
            pltpu.SemaphoreType.DMA((nz,)),
            pltpu.SemaphoreType.DMA((nz,)),
            pltpu.SemaphoreType.DMA((nz,)),
            pltpu.SemaphoreType.DMA,
        ],
        compiler_params=pltpu.CompilerParams(collective_id=cid, has_side_effects=True),
    )(own)


def line_exchange_kernel(nz, parts, out, send, recv, local_sem):
    dp, z = lax.axis_index("dp"), lax.axis_index("mp")
    barrier = pltpu.get_barrier_semaphore()
    for off in range(1, nz):
        pl.semaphore_signal(
            barrier, inc=1, device_id=(dp, lax.rem(z + off, nz)), device_id_type=MESH
        )
    keep = pltpu.make_async_copy(parts.at[z], out.at[z], local_sem)
    keep.start()
    pl.semaphore_wait(barrier, nz - 1)
    copies = []
    for off in range(1, nz):
        peer = lax.rem(z + off, nz)
        copy = pltpu.make_async_remote_copy(
            src_ref=parts.at[peer],
            dst_ref=out.at[z],
            send_sem=send.at[off],
            recv_sem=recv.at[off],
            device_id=(dp, peer),
            device_id_type=MESH,
        )
        copy.start()
        copies.append(copy)
    for copy in copies:
        copy.wait()
    keep.wait()


def line_exchange(parts, nz, cid):
    return pl.pallas_call(
        functools.partial(line_exchange_kernel, nz),
        out_shape=jax.ShapeDtypeStruct(parts.shape, parts.dtype),
        in_specs=[ANY],
        out_specs=ANY,
        scratch_shapes=[
            pltpu.SemaphoreType.DMA((nz,)),
            pltpu.SemaphoreType.DMA((nz,)),
            pltpu.SemaphoreType.DMA,
        ],
        compiler_params=pltpu.CompilerParams(collective_id=cid, has_side_effects=True),
    )(parts)


def joint_scatter_kernel(nd, nz, joint_cols, parts, out, vec, land, stage, zland, send, recv, zsend, zrecv):
    dp, z = lax.axis_index("dp"), lax.axis_index("mp")
    barrier = pltpu.get_barrier_semaphore()
    for off in range(1, nd):
        pl.semaphore_signal(
            barrier, inc=1, device_id=(lax.rem(dp + off, nd), z), device_id_type=MESH
        )
    for off in range(1, nz):
        pl.semaphore_signal(
            barrier, inc=1, device_id=(dp, lax.rem(z + off, nz)), device_id_type=MESH
        )
    pl.semaphore_wait(barrier, nd - 1 + nz - 1)
    copies = []
    for off in range(1, nd):
        peer = lax.rem(dp + off, nd)
        copy = pltpu.make_async_remote_copy(
            src_ref=parts.at[peer],
            dst_ref=land.at[off],
            send_sem=send.at[off],
            recv_sem=recv.at[off],
            device_id=(peer, z),
            device_id_type=MESH,
        )
        copy.start()
        copies.append(copy)
    total = parts[dp].astype(jnp.float32)
    for off, copy in zip(range(1, nd), copies):
        copy.wait_recv()
        total = total + land[off].astype(jnp.float32)
    rows = total.shape[0] // nz
    for j in range(nz):
        stage[j] = total[j * rows : (j + 1) * rows]
    zcopies = []
    for off in range(1, nz):
        peer = lax.rem(z + off, nz)
        copy = pltpu.make_async_remote_copy(
            src_ref=stage.at[peer],
            dst_ref=zland.at[z],
            send_sem=zsend.at[off],
            recv_sem=zrecv.at[off],
            device_id=(dp, peer),
            device_id_type=MESH,
        )
        copy.start()
        zcopies.append(copy)
    zland[z] = stage[z]
    for copy in zcopies:
        copy.wait_recv()
    sums = zland[0, :, joint_cols:]
    for j in range(1, nz):
        sums = sums + zland[j, :, joint_cols:]
    vec[...] = sums
    for j in range(nz):
        out[j] = zland[j, :, :joint_cols]
    for copy in copies:
        copy.wait_send()
    for copy in zcopies:
        copy.wait_send()


def joint_scatter(parts, joint_cols, nd, nz, cid):
    rows, cols = parts.shape[1:]
    own = rows // nz
    return pl.pallas_call(
        functools.partial(joint_scatter_kernel, nd, nz, joint_cols),
        out_shape=(
            jax.ShapeDtypeStruct((nz, own, joint_cols), jnp.float32),
            jax.ShapeDtypeStruct((own, cols - joint_cols), jnp.float32),
        ),
        in_specs=[VM],
        out_specs=(VM, VM),
        scratch_shapes=[
            pltpu.VMEM((nd, rows, cols), jnp.bfloat16),
            pltpu.VMEM((nz, own, cols), jnp.float32),
            pltpu.VMEM((nz, own, cols), jnp.float32),
            pltpu.SemaphoreType.DMA((nd,)),
            pltpu.SemaphoreType.DMA((nd,)),
            pltpu.SemaphoreType.DMA((nz,)),
            pltpu.SemaphoreType.DMA((nz,)),
        ],
        compiler_params=pltpu.CompilerParams(
            collective_id=cid, has_side_effects=True, vmem_limit_bytes=VMEM_LIMIT
        ),
    )(parts)


def attention_forward_kernel(qb, kc, nh, qkv, seg_row, seg_col, out, lse, bias, keys):
    seq = qkv.shape[1]
    for h in range(nh):
        keys[h] = qkv[(nh + h) * HD : (nh + h + 1) * HD, :].T

    def block(i, carry):
        start = pl.multiple_of(i * qb, qb)
        own_seg = seg_row[0:1, pl.ds(start, qb)]
        for c in range(0, seq, kc):
            bias[c : c + kc, :] = jnp.where(
                seg_col[c : c + kc, 0:1] == own_seg, 0.0, NEG_FILL
            )
        for h in range(nh):
            query = qkv[h * HD : (h + 1) * HD, pl.ds(start, qb)] * jnp.bfloat16(0.125)
            top = jnp.full((1, qb), -jnp.inf, jnp.float32)
            total = jnp.zeros((1, qb), jnp.float32)
            acc = jnp.zeros((HD, qb), jnp.float32)
            for c in range(0, seq, kc):
                score = nn(keys[h, c : c + kc, :], query) + bias[c : c + kc, :]
                new_top = jnp.maximum(top, jnp.max(score, axis=0, keepdims=True))
                weight = jnp.exp(score - new_top)
                fade = jnp.exp(top - new_top)
                total = total * fade + jnp.sum(weight, axis=0, keepdims=True)
                value = qkv[(2 * nh + h) * HD : (2 * nh + h + 1) * HD, c : c + kc]
                acc = acc * fade + nn(value, weight.astype(jnp.bfloat16))
                top = new_top
            out[h * HD : (h + 1) * HD, pl.ds(start, qb)] = acc / total
            lse[h : h + 1, pl.ds(start, qb)] = top + jnp.log(total)
        return carry

    lax.fori_loop(0, seq // qb, block, 0)


def attention_forward(qkv, seg_row, seg_col, nh):
    seq = qkv.shape[1]
    qb, kc = min(512, seq), min(1024, seq)
    return pl.pallas_call(
        functools.partial(attention_forward_kernel, qb, kc, nh),
        out_shape=(
            jax.ShapeDtypeStruct((nh * HD, seq), jnp.float32),
            jax.ShapeDtypeStruct((8, seq), jnp.float32),
        ),
        in_specs=[VM] * 3,
        out_specs=(VM, VM),
        scratch_shapes=[
            pltpu.VMEM((seq, qb), jnp.float32),
            pltpu.VMEM((nh, seq, HD), jnp.bfloat16),
        ],
        compiler_params=pltpu.CompilerParams(vmem_limit_bytes=VMEM_LIMIT),
    )(qkv, seg_row, seg_col)


def attention_backward_kernel(
    qb, kc, nh, qkv, grad, att, lse, seg_row, seg_col, out, bias, keys, values, key_grad, value_grad
):
    seq = qkv.shape[1]
    for h in range(nh):
        keys[h] = qkv[(nh + h) * HD : (nh + h + 1) * HD, :].T
        values[h] = qkv[(2 * nh + h) * HD : (2 * nh + h + 1) * HD, :].T
    key_grad[...] = jnp.zeros_like(key_grad)
    value_grad[...] = jnp.zeros_like(value_grad)

    def block(i, carry):
        start = pl.multiple_of(i * qb, qb)
        own_seg = seg_row[0:1, pl.ds(start, qb)]
        for c in range(0, seq, kc):
            bias[c : c + kc, :] = jnp.where(
                seg_col[c : c + kc, 0:1] == own_seg, 0.0, NEG_FILL
            )
        for h in range(nh):
            query = qkv[h * HD : (h + 1) * HD, pl.ds(start, qb)] * jnp.bfloat16(0.125)
            back = grad[h * HD : (h + 1) * HD, pl.ds(start, qb)]
            row_term = jnp.sum(
                back.astype(jnp.float32) * att[h * HD : (h + 1) * HD, pl.ds(start, qb)],
                axis=0,
                keepdims=True,
            )
            log_total = lse[h : h + 1, pl.ds(start, qb)]
            query_grad = jnp.zeros((HD, qb), jnp.float32)
            for c in range(0, seq, kc):
                chunk = slice(c, c + kc)
                score = nn(keys[h, chunk, :], query) + bias[chunk, :]
                weight = jnp.exp(score - log_total)
                value_grad[h, chunk, :] += nt(weight.astype(jnp.bfloat16), back)
                weight_grad = nn(values[h, chunk, :], back)
                score_grad = (weight * (weight_grad - row_term)).astype(jnp.bfloat16)
                key_grad[h, chunk, :] += nt(score_grad, query)
                query_grad = query_grad + nn(
                    qkv[(nh + h) * HD : (nh + h + 1) * HD, chunk], score_grad
                )
            out[h * HD : (h + 1) * HD, pl.ds(start, qb)] = (query_grad * 0.125).astype(
                jnp.bfloat16
            )
        return carry

    lax.fori_loop(0, seq // qb, block, 0)
    for h in range(nh):
        out[(nh + h) * HD : (nh + h + 1) * HD, :] = key_grad[h].T.astype(jnp.bfloat16)
        out[(2 * nh + h) * HD : (2 * nh + h + 1) * HD, :] = value_grad[h].T.astype(jnp.bfloat16)


def attention_backward(qkv, grad, att, lse, seg_row, seg_col, nh):
    seq = qkv.shape[1]
    qb, kc = min(512, seq), min(512, seq)
    return pl.pallas_call(
        functools.partial(attention_backward_kernel, qb, kc, nh),
        out_shape=jax.ShapeDtypeStruct((3 * nh * HD, seq), jnp.bfloat16),
        in_specs=[VM] * 6,
        out_specs=VM,
        scratch_shapes=[
            pltpu.VMEM((seq, qb), jnp.float32),
            pltpu.VMEM((nh, seq, HD), jnp.bfloat16),
            pltpu.VMEM((nh, seq, HD), jnp.bfloat16),
            pltpu.VMEM((nh, seq, HD), jnp.float32),
            pltpu.VMEM((nh, seq, HD), jnp.float32),
        ],
        compiler_params=pltpu.CompilerParams(vmem_limit_bytes=VMEM_LIMIT),
    )(qkv, grad, att, lse, seg_row, seg_col)


def local(
    tokens,
    segments,
    out_grad,
    align_grad,
    first_gain,
    first_shift,
    joint_weight,
    query_bias,
    value_bias,
    output_weight,
    output_bias,
    second_gain,
    second_shift,
    expand_bias,
    reduce_bias,
    head_gain,
    head_shift,
    align_weight,
    align_bias,
    expand_weight,
    reduce_weight,
):
    nd, nz = lax.axis_size("dp"), lax.axis_size("mp")
    n = nd * nz
    z = lax.axis_index("mp")
    rows, width = tokens.shape
    seq = rows * nz
    nh = H // nz
    own_cols = nh * HD
    f32, b16 = jnp.float32, jnp.bfloat16

    shards = [
        joint_weight,
        output_weight,
        align_weight,
        expand_weight,
        reduce_weight.T,
        first_gain,
        first_shift,
        query_bias,
        value_bias,
        output_bias,
        second_gain,
        second_shift,
        reduce_bias,
        head_gain,
        head_shift,
        expand_bias,
        align_bias,
    ]
    own_size = sum(s.size for s in shards)
    lines = -(-own_size // (16 * width)) * 16
    filler = jnp.zeros((lines * width - own_size,), b16)
    packed = jnp.concatenate([s.reshape(-1) for s in shards] + [filler])
    packed = lax.all_gather(packed.reshape(lines, width), ("dp", "mp"), axis=0, tiled=True)
    packed = packed.reshape(n, lines * width)
    full, at = [], 0
    for s in shards:
        full.append(packed[:, at : at + s.size].reshape((n,) + s.shape))
        at += s.size
    joint_full = full[0].reshape(width, 3 * width)
    output_full = full[1].reshape(width, width)
    align_full = full[2].reshape(width, -1)

    def spread(parts):
        a, b = parts.shape[1:]
        return parts.reshape(nd, nz, a, b).transpose(0, 2, 1, 3).reshape(nd * a, nz * b)

    expand_full = spread(full[3])
    reduce_full = spread(full[4])
    (
        gain_one,
        shift_one,
        bias_query,
        bias_value,
        bias_output,
        gain_two,
        shift_two,
        bias_reduce,
        gain_head,
        shift_head,
        bias_expand,
        bias_align,
    ) = (v.reshape(-1).astype(f32) for v in full[5:])

    x_all = line_gather(tokens, nz, 1).reshape(seq, width)
    normed_all = layer_norm(x_all.astype(f32), gain_one, shift_one).astype(b16)
    joint_own = lax.dynamic_slice_in_dim(
        joint_full.reshape(width, 3, width), z * own_cols, own_cols, axis=2
    ).reshape(width, 3 * own_cols)
    joint_bias = jnp.stack([bias_query, jnp.zeros_like(bias_query), bias_value])
    bias_own = lax.dynamic_slice_in_dim(joint_bias, z * own_cols, own_cols, axis=1).reshape(-1)
    qkv = (
        jnp.einsum("ic,ri->cr", joint_own, normed_all, preferred_element_type=f32)
        + bias_own[:, None]
    ).astype(b16)
    seg_row, seg_col = segments.reshape(1, seq), segments.reshape(seq, 1)
    att, lse = attention_forward(qkv, seg_row, seg_col, nh)
    att_parts = att.astype(b16).reshape(own_cols, nz, rows).transpose(1, 0, 2)
    attended = line_exchange(att_parts, nz, 2).reshape(width, rows)

    resid = tokens.astype(f32)
    middle = (
        resid
        + jnp.einsum("ir,io->ro", attended, output_full, preferred_element_type=f32)
        + bias_output
    )
    normed_two = layer_norm(middle, gain_two, shift_two).astype(b16)
    preactivation = matmul(normed_two, expand_full) + bias_expand
    activated = exact_gelu(preactivation).astype(b16)
    block_out = middle + right_product(activated, reduce_full) + bias_reduce
    normed_three = layer_norm(block_out, gain_head, shift_head).astype(b16)
    align_out = matmul(normed_three, align_full) + bias_align
    grad_align_w = left_product(normed_three, align_grad)
    grad_align_b = column_sums(align_grad)
    back_three = right_product(align_grad, align_full)
    _, norm_pull = jax.vjp(layer_norm, block_out, gain_head, shift_head)
    back_extra, grad_head_gain, grad_head_shift = norm_pull(back_three)
    back_block = out_grad.astype(f32) + back_extra
    back_feed = back_block.astype(b16)
    grad_reduce_b = column_sums(back_feed)
    grad_reduce_w = left_product(back_feed, activated)
    back_active = matmul(back_feed, reduce_full)
    _, gelu_pull = jax.vjp(exact_gelu, preactivation)
    back_pre = gelu_pull(back_active)[0].astype(b16)
    grad_expand_w = left_product(normed_two, back_pre)
    grad_expand_b = column_sums(back_pre)
    back_two = right_product(back_pre, expand_full)
    _, norm_pull = jax.vjp(layer_norm, middle, gain_two, shift_two)
    middle_extra, grad_second_gain, grad_second_shift = norm_pull(back_two)
    back_middle = back_block + middle_extra
    back_output = back_middle.astype(b16)
    grad_output_b = column_sums(back_output)
    grad_output_w = jnp.einsum("ir,ro->io", attended, back_output, preferred_element_type=f32)
    back_att = jnp.einsum(
        "io,ro->ir", output_full, back_output, preferred_element_type=f32
    ).astype(b16)

    def gather_order(grad, a, b):
        return grad.reshape(nd, a, nz, b).transpose(0, 2, 1, 3).reshape(n, a * b)

    pieces = [
        grad_output_w.reshape(n, -1),
        grad_align_w.reshape(n, -1),
        gather_order(grad_expand_w, *expand_weight.shape),
        gather_order(grad_reduce_w, *reduce_weight.shape[::-1]),
        grad_output_b.reshape(n, -1),
        grad_second_gain.reshape(n, -1),
        grad_second_shift.reshape(n, -1),
        grad_reduce_b.reshape(n, -1),
        grad_head_gain.reshape(n, -1),
        grad_head_shift.reshape(n, -1),
        grad_expand_b.reshape(n, -1),
        grad_align_b.reshape(n, -1),
    ]
    own_size = sum(p.shape[1] for p in pieces)
    lines = -(-own_size // (16 * width)) * 16
    pieces.append(jnp.zeros((n, lines * width - own_size), f32))
    scattered = lax.psum_scatter(
        jnp.concatenate([p.astype(b16) for p in pieces], axis=1).reshape(n * lines, width),
        ("dp", "mp"),
        scatter_dimension=0,
        tiled=True,
    ).reshape(-1)
    got, at = [], 0
    for p in pieces:
        got.append(scattered[at : at + p.shape[1]].astype(f32))
        at += p.shape[1]

    grad_att = line_exchange(back_att.reshape(nz, own_cols, rows), nz, 3)
    grad_att = grad_att.transpose(1, 0, 2).reshape(own_cols, seq)
    back_joint = attention_backward(qkv, grad_att, att, lse, seg_row, seg_col, nh)
    joint_parts = back_joint.reshape(3 * own_cols, nz, rows).transpose(1, 0, 2)
    back_rows = line_exchange(joint_parts, nz, 4)
    back_rows = (
        back_rows.reshape(nz, 3, own_cols, rows).transpose(1, 0, 2, 3).reshape(3 * width, rows)
    )
    back_one = jnp.einsum("cr,ic->ri", back_rows, joint_full, preferred_element_type=f32)
    _, norm_pull = jax.vjp(layer_norm, resid, gain_one, shift_one)
    input_extra, grad_first_gain, grad_first_shift = norm_pull(back_one)
    tokens_grad = back_middle + input_extra
    grad_joint = jnp.einsum("ri,cr->ic", normed_all, back_joint, preferred_element_type=f32)
    sums = jnp.sum(back_joint.astype(f32), axis=1).reshape(3, own_cols)
    zero = jnp.zeros((width,), f32)
    grad_query_b = lax.dynamic_update_slice_in_dim(zero, sums[0], z * own_cols, 0)
    grad_value_b = lax.dynamic_update_slice_in_dim(zero, sums[2], z * own_cols, 0)
    vectors = jnp.stack([grad_first_gain, grad_first_shift, grad_query_b, grad_value_b], axis=1)
    pad = -(3 * own_cols + 4) % 128
    parts = jnp.concatenate(
        [grad_joint, vectors, jnp.zeros((width, pad), f32)], axis=1
    ).astype(b16)
    joint_mine, vec_mine = joint_scatter(
        parts.reshape(nd, width // nd, -1), 3 * own_cols, nd, nz, 5
    )
    g_joint = (
        joint_mine.reshape(nz, -1, 3, own_cols).transpose(1, 2, 0, 3).reshape(-1, 3 * width)
    )
    return (
        block_out.astype(b16),
        align_out.astype(b16),
        tokens_grad,
        vec_mine[:, 0],
        vec_mine[:, 1],
        g_joint,
        vec_mine[:, 2],
        vec_mine[:, 3],
        got[0].reshape(output_weight.shape),
        got[4],
        got[5],
        got[6],
        got[10],
        got[7],
        got[8],
        got[9],
        got[1].reshape(align_weight.shape),
        got[11],
        got[2].reshape(expand_weight.shape),
        got[3].reshape(reduce_weight.shape[::-1]).T,
    )


def solution(mesh):
    both = P(("dp", "mp"))
    rows = P(("dp", "mp"), None)
    in_specs = (
        (rows, P("dp", None), rows, rows, both, both, rows, both, both, rows)
        + (both,) * 7
        + (rows, both, P("dp", "mp"), P("mp", "dp"))
    )
    out_specs = (
        (rows, rows, rows, both, both, rows, both, both, rows)
        + (both,) * 7
        + (rows, both, P("dp", "mp"), P("mp", "dp"))
    )
    return jax.shard_map(local, mesh=mesh, in_specs=in_specs, out_specs=out_specs, check_vma=False)
```

time: 1390 us -> 659 us (0.47)
  waiting for transfers between devices: 876 us -> 10.5 us
  Pallas kernels: 0 us -> 315 us
  matrix products: 258 us -> 71.3 us
  local copies, waits for them, and re-layouts: 94 us -> 202 us
  blocking collectives: 84.6 us -> 0 us
  other arithmetic: 56.6 us -> 36.2 us
    reduce_scatter x9 -> x1, waiting for transfers between devices: 569 us -> 0.01 us  [local(): lax.psum_scatter(jnp.concatenate([p.astype(b16) for p in pieces], axis=1)...]
    pallas_call x0 -> x7, Pallas kernels: none -> 315 us  [the longest x1 123 us: line_gather(): pl.pallas_call(functools.partial(line_gather_kernel, nz), out_shape=jax.S...]
    all_gather x8 -> x1, waiting for transfers between devices: 303 us -> 10.4 us  [local(): lax.all_gather(packed.reshape(lines, width), ('dp', 'mp'), axis=0, tiled=...]
    dot_general x28 -> x6, matrix products: 169 us -> 19.9 us  [the longest x1 5.49 us: local(): jnp.einsum('ri,cr->ic', normed_all, back_joint, preferred_element_type=f32)]
    unnamed x2 -> x0, blocking collectives: 84.6 us -> none
    reshape x2 -> x15, local copies, waits for them, and re-layouts: 12.4 us -> 43.7 us  [the longest x1 14.9 us: local(): packed = packed.reshape(n, lines * width)]
    reduce_sum x4 -> x1, other arithmetic: 28.8 us -> 2.21 us  [local(): sums = jnp.sum(back_joint.astype(f32), axis=1).reshape(3, own_cols)]
    another operation x1 -> x9, local copies, waits for them, and re-layouts: 0.01 us -> 25.9 us  [the longest x1 7.74 us: local(): joint_full.reshape(width, 3, width)]
  transfers between devices with their start and end apart: 17 -> 2, of which waited for: 15 -> 1; matrix products, arithmetic and copies ran while one was open for 16% -> 9% of each run, Pallas kernels for 0% -> 42%
where the time goes in v1:
time: 659 us; the launch traced here: 651 us
  Pallas kernels  315 us (48%)
  local copies, waits for them, and re-layouts  202 us (31%)
  matrix products  71.3 us (11%)
  other arithmetic  36.2 us (5%)
  between operations  15 us (2%)
  waiting for transfers between devices  10.5 us (2%)
    pallas_call x1, Pallas kernels, line_gather(): pl.pallas_call(functools.partial(line_gather_kernel, nz), out_shape=jax.S...  123 us
    pallas_call x3, Pallas kernels, line_exchange(): pl.pallas_call(functools.partial(line_exchange_kernel, nz), out_shape=jax...  88 us
    unnamed x111, local copies, waits for them, and re-layouts  43.1 us
    pallas_call x1, Pallas kernels, joint_scatter(): pl.pallas_call(functools.partial(joint_scatter_kernel, nd, nz, joint_cols...  40 us
    pallas_call x1, Pallas kernels, attention_backward(): pl.pallas_call(functools.partial(attention_backward_kernel, qb, kc, nh),...  38.1 us
    convert_element_type x14, local copies, waits for them, and re-layouts, local(): p.astype(b16)  32.6 us
    dot_general x3, matrix products, matmul(): return jnp.dot(left, right, preferred_element_type=jnp.float32)  30.3 us
    pallas_call x1, Pallas kernels, attention_forward(): pl.pallas_call(functools.partial(attention_forward_kernel, qb, kc, nh), o...  26.4 us
  transfers between devices with their start and end apart: 2, of which 1 were waited for; matrix products, arithmetic and copies ran while one was open for 9% of the time, Pallas kernels for 42%

profile of v1, /device:TPU:0, one launch (start us, length us, event | category | flops | bytes accessed | tf_op | source)
XLA Modules:
  0.0 650.6 jit_solution(6161332979972461563)
XLA Ops:
  12.2 11.6 %concatenate.19 = bf16[258048]{0:T(1024)(128)(2,1)S(1)} concatenate(bf16[55296]{0:T(1024)(128)(2,1)S(1)} %reshape.427, bf16[18432]{0:T(1024)(128)(2,1)S(1)} %reshape.428, bf16[24576]{0:T(1024)(128)(2,1)S(1)} %bitcast.151, bf16[73728]{0:T(1024)(128)(2,1)S(1)} %reshape.430, bf16[73728]{0:T(1024)(128)(2,1)S(1)} %reshape.431, bf16[24]{0:T(256)(128)(2,1)} %param.25, ...), dimensions={0} | concatenate | bytes 1032192 | tf_op jit(solution)/shard_map/concatenate | solution.py:450
  27.3 122.7 %shard_map.356 = bf16[4,512,768]{2,1,0:T(8,128)(2,1)} custom-call(bf16[512,768]{1,0:T(8,128)(2,1)} %own.1), custom_call_target="tpu_custom_call" | custom-call | tf_op jit(solution)/shard_map/pallas_call | solution.py:132
  155.0 10.4 %all-gather.2.cloned.1.call-done = bf16[10752,768]{1,0:T(8,128)(2,1)} async-done(((bf16[336,768]{1,0:T(8,128)(2,1)}), bf16[10752,768]{1,0:T(8,128)(2,1)}) %all-gather.2.cloned.1.call-update) | async-done | bytes 16515088 | tf_op jit(solution)/shard_map/all_gather | solution.py:451
  165.4 14.9 %reshape.433 = bf16[32,258048]{1,0:T(8,128)(2,1)} reshape(bf16[10752,768]{1,0:T(8,128)(2,1)} %all-gather.2.cloned.1.call-done) | data formatting | bytes 33030144 | tf_op jit(solution)/shard_map/reshape | solution.py:452
  191.3 7.9 %fusion.44 = (bf16[32,73728]{1,0:T(8,128)(2,1)}, bf16[32,73728]{1,0:T(8,128)(2,1)}) fusion(bf16[32,258048]{1,0:T(8,128)(2,1)} %reshape.433), kind=kLoop, calls=%fused_computation.136 | loop fusion | bytes 18874368 | tf_op jit(solution)/shard_map/slice | solution.py:455
  224.2 7.7 %reshape_reshape_reshape.3 = bf16[768,3,768]{2,1,0:T(4,128)(2,1)} reshape(bf16[32,55296]{1,0:T(8,128)(2,1)} %slice.146) | data formatting | bytes 7077888 | tf_op jit(solution)/shard_map/reshape;reshape;reshape | solution.py:485
  231.9 4.1 constant_dynamic-slice_fusion
  244.2 26.4 %shard_map.357 = (f32[192,2048]{1,0:T(8,128)}, f32[8,2048]{1,0:T(8,128)}) custom-call(bf16[576,2048]{1,0:T(8,128)(2,1)} %add_convert_fusion.2.qkv, s32[1,2048]{1,0:T(1,128)} %seg_row.3, s32[2048,1]{1,0:T(8,128)} %copy.61.seg_col), custom_call_target="tpu_custom_call" | custom-call | tf_op jit(solution)/shard_map/pallas_call | solution.py:312
  273.1 17.5 %shard_map.358 = bf16[4,192,512]{2,1,0:T(8,128)(2,1)} custom-call(bf16[4,192,512]{2,1,0:T(8,128)(2,1)} %bitcast.144), custom_call_target="tpu_custom_call" | custom-call | tf_op jit(solution)/shard_map/pallas_call | solution.py:176
  293.7 20.0 %multiply_convert_fusion = (bf16[512,3072]{1,0:T(8,128)(2,1)S(1)}, f32[512,3072]{1,0:T(8,128)}, f32[512,3072]{1,0:T(8,128)}) fusion(f32[3072]{0:T(1024)S(1)} %reshape.456, bf16[768,3072]{1,0:T(8,128)(2,1)} %bitcast.131, f32[512,768]{1,0:T(8,128)S(1)} %get-tuple-element.84, f32[768]{0:T(1024)S(1)} %reshape.455, f32[768]{0:T(1024)S(1)} %reshape.454, ...), kind=kOutput, calls=%fused_computation.8 | convolution fusion | flops 2521694208 | bytes 22042624 | tf_op jit(solution)/shard_map/dot_general | solution.py:29
  321.1 8.2 %fusion.38 = (bf16[3072]{0:T(1024)(128)(2,1)S(1)}, bf16[512,3072]{1,0:T(8,128)(2,1)S(1)}) fusion(f32[512,3072]{1,0:T(8,128)} %get-tuple-element.53, f32[512,3072]{1,0:T(8,128)} %get-tuple-element.85, f32[3072]{0:T(1024)S(1)} %reshape.456, bf16[512,768]{1,0:T(8,128)(2,1)S(1)} %get-tuple-element.45, bf16[768,3072]{1,0:T(8,128)(2,1)S(1)} %bitcast.138), kind=kOutput, calls=%fused_computation.132 | convolution fusion | flops 2441081856 | bytes 21252096 | tf_op jit(solution)/shard_map/dot_general | solution.py:29
  333.4 4.8 convolution_convert_fusion.1
  338.2 4.3 convolution_convert_fusion
  351.2 9.9 %convert_element_type.361 = bf16[8,96,4,768]{3,2,1,0:T(4,128)(2,1)} reshape(bf16[768,3072]{1,0:T(8,128)(2,1)} %convolution_convert_fusion.1) | data formatting | bytes 9437184 | tf_op jit(solution)/shard_map/convert_element_type | solution.py:556
  364.4 4.8 copy.87
  381.0 9.7 %convert_element_type.365 = bf16[8,96,4,768]{3,2,1,0:T(4,128)(2,1)} reshape(bf16[768,3072]{1,0:T(8,128)(2,1)} %convolution_convert_fusion) | data formatting | bytes 9437184 | tf_op jit(solution)/shard_map/convert_element_type | solution.py:556
  420.3 12.0 %reshape.447 = bf16[8192,768]{1,0:T(8,128)(2,1)} reshape(bf16[32,196608]{1,0:T(8,128)(2,1)} %dynamic-update-slice.12) | data formatting | bytes 25165824 | tf_op jit(solution)/shard_map/reshape | solution.py:556
  434.3 5.1 reshape_reshape.19
  443.4 4.9 copy.69
  450.0 19.7 %shard_map.359 = bf16[4,192,512]{2,1,0:T(8,128)(2,1)} custom-call(bf16[4,192,512]{2,1,0:T(8,128)(2,1)} %bitcast.150), custom_call_target="tpu_custom_call" | custom-call | tf_op jit(solution)/shard_map/pallas_call | solution.py:176
  471.8 38.1 %shard_map.360 = bf16[576,2048]{1,0:T(8,128)(2,1)} custom-call(bf16[576,2048]{1,0:T(8,128)(2,1)} %add_convert_fusion.2.qkv, bf16[192,2048]{1,0:T(8,128)(2,1)} %bitcast.141, f32[192,2048]{1,0:T(8,128)} %get-tuple-element.24.att, f32[8,2048]{1,0:T(8,128)} %get-tuple-element.25.lse, s32[1,2048]{1,0:T(1,128)} %seg_row.3, s32[2048,1]{1,0:T(8,128)} %copy.61.seg_col), custom_call_target="tpu_custom_call" | custom-call | tf_op jit(solution)/shard_map/pallas_call | solution.py:380
  515.1 50.9 %shard_map.361 = bf16[4,576,512]{2,1,0:T(8,128)(2,1)} custom-call(bf16[4,576,512]{2,1,0:T(8,128)(2,1)} %bitcast.130), custom_call_target="tpu_custom_call" | custom-call | tf_op jit(solution)/shard_map/pallas_call | solution.py:176
  577.7 5.5 fusion.22
  586.7 40.0 %shard_map.362 = (f32[4,24,576]{2,1,0:T(8,128)}, f32[24,64]{1,0:T(8,128)}) custom-call(bf16[8,96,640]{2,1,0:T(8,128)(2,1)} %concatenate.24.parts), custom_call_target="tpu_custom_call" | custom-call | tf_op jit(solution)/shard_map/pallas_call | solution.py:253
  (235 shorter events, 174.5 us)
Async XLA Ops:
  7.2 17.9 %copy-start.20 = (bf16[512,1024]{1,0:T(8,128)(2,1)S(1)}, bf16[512,1024]{1,0:T(8,128)(2,1)}, u32[]{:S(2)}) copy-start(bf16[512,1024]{1,0:T(8,128)(2,1)} %param.24) | copy-start | bytes 3145732
  7.2 18.7 %copy-start.23 = (s32[1,2048]{1,0:T(1,128)S(1)}, s32[1,2048]{1,0:T(1,128)}, u32[]{:S(2)}) copy-start(s32[1,2048]{1,0:T(1,128)} %seg_row.3) | copy-start | bytes 24580
  7.2 158.2 %all-gather.2.cloned.1.call-start = ((), (), s32[]{:S(2)}) async-start(), calls=%async_computation.1 | async-start | bytes 17031168 | tf_op jit(solution)/shard_map/all_gather | solution.py:451
  25.0 610.8 %reduce-scatter.2.cloned.1.call-start = ((), (), s32[]{:S(2)}) async-start(), calls=%async_computation.2 | async-start | bytes 12976128 | tf_op jit(solution)/shard_map/reduce_scatter | solution.py:555
  199.4 145.0 %copy-start.29 = (f32[768]{0:T(1024)}, f32[768]{0:T(1024)S(1)}, u32[]{:S(2)}) copy-start(f32[768]{0:T(1024)S(1)} %reshape.458) | copy-start | bytes 9220
  290.6 23.1 %slice-start.6 = ((s8[4718592]{0:T(1024)(128)(4,1)}), s8[4194304]{0:T(1024)(128)(4,1)S(1)}, s32[]{:S(2)}) async-start(s8[4718592]{0:T(1024)(128)(4,1)} %bitcast.135), calls=%async_computation.9 | async-start | bytes 8388608
  293.4 40.0 %copy-start.9 = (f32[512,768]{1,0:T(8,128)}, f32[512,768]{1,0:T(8,128)S(1)}, u32[]{:S(2)}) copy-start(f32[512,768]{1,0:T(8,128)S(1)} %get-tuple-element.84) | copy-start | bytes 4718596
  293.7 20.0 %slice-start.7 = ((s8[4718592]{0:T(1024)(128)(4,1)}), s8[524288]{0:T(1024)(128)(4,1)S(1)}, s32[]{:S(2)}) async-start(s8[4718592]{0:T(1024)(128)(4,1)} %bitcast.135), calls=%async_computation.10 | async-start | bytes 1048576
  316.8 27.6 %copy-start.31 = (f32[512]{0:T(512)}, f32[512]{0:T(512)S(1)}, u32[]{:S(2)}) copy-start(f32[512]{0:T(512)S(1)} %fusion.29) | copy-start | bytes 6148
  320.8 8.6 %slice-start.4 = ((s8[4718592]{0:T(1024)(128)(4,1)}), s8[4194304]{0:T(1024)(128)(4,1)S(1)}, s32[]{:S(2)}) async-start(s8[4718592]{0:T(1024)(128)(4,1)} %bitcast.132), calls=%async_computation.7 | async-start | bytes 8388608
  321.1 8.3 %slice-start.5 = ((s8[4718592]{0:T(1024)(128)(4,1)}), s8[524288]{0:T(1024)(128)(4,1)S(1)}, s32[]{:S(2)}) async-start(s8[4718592]{0:T(1024)(128)(4,1)} %bitcast.132), calls=%async_computation.8 | async-start | bytes 1048576
  342.6 5.8 copy-start.34
  393.9 5.9 slice-start
  394.0 5.8 slice-start.1
  402.3 12.8 %copy-start.24 = (bf16[32,32]{1,0:T(8,128)(2,1)S(1)}, bf16[32,32]{1,0:T(8,128)(2,1)}, u32[]{:S(2)}) copy-start(bf16[32,32]{1,0:T(8,128)(2,1)} %convert_element_type.379) | copy-start | bytes 6148
  443.3 4.9 copy-start.2
  443.4 4.9 copy-start.19
  583.2 47.3 %copy-start.33 = (f32[512]{0:T(512)S(1)}, f32[512]{0:T(512)}, u32[]{:S(2)}) copy-start(f32[512]{0:T(512)} %get-tuple-element.33) | copy-start | bytes 6148
  583.2 47.3 %copy-start.3 = (f32[512,768]{1,0:T(8,128)S(1)}, f32[512,768]{1,0:T(8,128)}, u32[]{:S(2)}) copy-start(f32[512,768]{1,0:T(8,128)} %get-tuple-element.47) | copy-start | bytes 4718596
  583.2 47.3 %copy-start.28 = (f32[512]{0:T(512)S(1)}, f32[512]{0:T(512)}, u32[]{:S(2)}) copy-start(f32[512]{0:T(512)} %copy-done.27) | copy-start | bytes 6148
  628.0 5.7 copy-start.30
  628.0 5.7 copy-start.32
  628.0 5.7 copy-start.35
  628.0 5.7 copy-start.36
  (23 other events, 63.3 us)
Sparse Core Ops, SparseCore 0:
  25.1 140.2 all-gather.1
  432.4 183.5 reduce-scatter.1
